TPU v7x, 256 devices: a whole 4x4x8 slice. The times are simulated.
256 devices in a mesh: seq: 32 (over y_hi, z, core), chan: 8 (over y_lo, x).
Axes of the slice: x: 4, y: 4 (y_hi: 2, y_lo: 2; y = y_hi * 2 + y_lo), z: 8, core: 2. Of those that a mesh axis runs over, the one named last changes fastest.
Arguments:
- proj: bfloat16 [3, 16384, 8192], P(None, 'seq', 'chan'), may hold values from -64 to 64
- short_weight: float32 [3, 7, 8192], P(None, None, 'chan'), may hold values from -40 to 40
- spectrum: bfloat16 [2, 64, 512, 8192], P(None, 'seq', None, 'chan'), as said below
- skip: float32 [8192], P('chan'), may hold values from 0.3 to 1.5
- gain: float32 [8192], P('chan'), may hold values from 0.5 to 1.5
Outputs:
- mixer_out: bfloat16 [32, 2, 256, 8192], P('seq', None, None, 'chan')
Inputs may be any that keep to these rules, and one draw needn't show every extreme that they name: `spectrum`: the transform of a real causal filter per channel whose values at lags 16384 and beyond are zero.
All inputs are finite; a program needn't handle non-finite values.
Results may differ from a plain program's by a relative error of at most 0.0065.
Values may be sent and summed in bfloat16 or wider, within the bound.
A program may use at most 128 MiB of HBM per device.

v0:
```python
import math

import jax
import jax.numpy as jnp
from jax import lax
from jax.sharding import PartitionSpec as P

D = 8192


epsilon = 1e-05


def passed_along(value, axis, steps):
    count = lax.axis_size(axis)
    initial, last = (max(0, -steps), min(count, count - steps))
    return lax.ppermute(value, axis, [(source, source + steps) for source in range(initial, last)])


def dft_table(out_count, in_count, period, direction):
    product_index = (
        jnp.arange(out_count, dtype=jnp.int32)[:, None]
        * jnp.arange(in_count, dtype=jnp.int32)[None, :]
        % period
    )
    angle = product_index.astype(jnp.float32) * (direction * 2.0 * math.pi / period)
    return (jnp.cos(angle).astype(jnp.bfloat16), jnp.sin(angle).astype(jnp.bfloat16))


def twiddle_table(freq_index, place_index, span_size, direction):
    product_index = freq_index[:, None] * place_index[None, :]
    angle = product_index.astype(jnp.float32) * (direction * 2.0 * math.pi / span_size)
    return (jnp.cos(angle), jnp.sin(angle))


def short_filters(proj, short_weight):
    taps = short_weight.shape[1]
    local_rows = proj.shape[1]
    before = passed_along(proj[:, local_rows - (taps - 1) :, :], "seq", 1)
    extended = jnp.concatenate([before, proj], axis=1)
    shorts = jnp.zeros(proj.shape, jnp.float32)
    for tap_index in range(taps):
        offset = taps - 1 - tap_index
        shorts = (
            shorts
            + short_weight[:, tap_index, None, :] * extended[:, offset : offset + local_rows, :]
        )
    return (shorts[0].astype(jnp.bfloat16), (shorts[1] * shorts[2]).astype(jnp.bfloat16))


def body(proj, short_weight, spectrum, skip, gain):
    gate, gated = short_filters(proj, short_weight)
    shard_count = lax.axis_size("seq")
    my_shard = lax.axis_index("seq")
    local_rows = proj.shape[1]
    local_width = proj.shape[2]
    half_rows = local_rows // 2
    span_size = 2 * shard_count * local_rows
    outer_cos, outer_sin = dft_table(2 * shard_count, shard_count, 2 * shard_count, -1.0)
    inner_cos, inner_sin = dft_table(local_rows, local_rows, local_rows, -1.0)
    back_cos, back_sin = dft_table(shard_count, 2 * shard_count, 2 * shard_count, 1.0)
    piece_rows = local_rows // shard_count
    columns = lax.all_to_all(
        jnp.stack([gated, gate])[:, None], "seq", split_axis=2, concat_axis=1, tiled=True
    )
    gated_cols = columns[0]
    gate_cols = columns[1]
    part_re = jnp.einsum("kn,nmc->kmc", outer_cos, gated_cols, preferred_element_type=jnp.float32)
    part_im = jnp.einsum("kn,nmc->kmc", outer_sin, gated_cols, preferred_element_type=jnp.float32)
    place_index = my_shard * piece_rows + jnp.arange(piece_rows, dtype=jnp.int32)
    turn_cos, turn_sin = twiddle_table(
        jnp.arange(2 * shard_count, dtype=jnp.int32), place_index, span_size, -1.0
    )
    turn_cos = turn_cos[:, :, None]
    turn_sin = turn_sin[:, :, None]
    first = jnp.stack(
        [
            (turn_cos * part_re - turn_sin * part_im).astype(jnp.bfloat16),
            (turn_cos * part_im + turn_sin * part_re).astype(jnp.bfloat16),
        ]
    )
    spectral = lax.all_to_all(first, "seq", split_axis=1, concat_axis=2, tiled=True)
    freq_re = jnp.einsum(
        "jm,kmc->kjc", inner_cos, spectral[0], preferred_element_type=jnp.float32
    ) - jnp.einsum("jm,kmc->kjc", inner_sin, spectral[1], preferred_element_type=jnp.float32)
    freq_im = jnp.einsum(
        "jm,kmc->kjc", inner_cos, spectral[1], preferred_element_type=jnp.float32
    ) + jnp.einsum("jm,kmc->kjc", inner_sin, spectral[0], preferred_element_type=jnp.float32)
    filtered_re = (spectrum[0] * freq_re - spectrum[1] * freq_im).astype(jnp.bfloat16)
    filtered_im = (spectrum[0] * freq_im + spectrum[1] * freq_re).astype(jnp.bfloat16)
    spread_re = jnp.einsum(
        "jm,kjc->kmc", inner_cos, filtered_re, preferred_element_type=jnp.float32
    ) + jnp.einsum("jm,kjc->kmc", inner_sin, filtered_im, preferred_element_type=jnp.float32)
    spread_im = jnp.einsum(
        "jm,kjc->kmc", inner_cos, filtered_im, preferred_element_type=jnp.float32
    ) - jnp.einsum("jm,kjc->kmc", inner_sin, filtered_re, preferred_element_type=jnp.float32)
    freq_index = 2 * my_shard + jnp.arange(2, dtype=jnp.int32)
    return_cos, return_sin = twiddle_table(
        freq_index, jnp.arange(local_rows, dtype=jnp.int32), span_size, -1.0
    )
    return_cos = return_cos[:, :, None]
    return_sin = return_sin[:, :, None]
    returned = jnp.stack(
        [
            (return_cos * spread_re + return_sin * spread_im).astype(jnp.bfloat16),
            (return_cos * spread_im - return_sin * spread_re).astype(jnp.bfloat16),
        ]
    )
    columns_back = lax.all_to_all(returned, "seq", split_axis=2, concat_axis=1, tiled=True)
    long_conv = (
        jnp.einsum("nk,kmc->nmc", back_cos, columns_back[0], preferred_element_type=jnp.float32)
        - jnp.einsum("nk,kmc->nmc", back_sin, columns_back[1], preferred_element_type=jnp.float32)
    ) * (1.0 / span_size)
    mixed = gate_cols.astype(jnp.float32) * (long_conv + skip * gated_cols.astype(jnp.float32))
    power = lax.psum(jnp.sum(mixed * mixed, axis=-1), "chan") / D
    normed = (mixed * lax.rsqrt(power + epsilon)[:, :, None] * gain).astype(jnp.bfloat16)
    upper_half = (my_shard >= shard_count // 2).astype(jnp.int32)
    target = jnp.arange(shard_count, dtype=jnp.int32)
    order = jnp.where(
        target % 2 == upper_half,
        (target - upper_half) // 2,
        (2 * shard_count - 1 - target - upper_half) // 2,
    )
    received = lax.all_to_all(
        jnp.take(normed, order, axis=0), "seq", split_axis=0, concat_axis=0, tiled=True
    )
    halves = received.reshape(2, half_rows, local_width)
    return jnp.where(my_shard % 2 == 0, halves, halves[::-1])[None]


def solution(mesh):
    placed = (
        P(None, "seq", "chan"),
        P(None, None, "chan"),
        P(None, "seq", None, "chan"),
        P("chan"),
        P("chan"),
    )
    return jax.shard_map(
        body, mesh=mesh, in_specs=placed, out_specs=P("seq", None, None, "chan"), check_vma=False
    )
```

profile of v0, /device:TPU:1, one launch (start us, length us, event | category | flops | bytes accessed | tf_op | source)
XLA Modules:
  0.0 481.1 jit_solution(15987562593052376782)
XLA Ops:
  0.8 4.9 %collective-permute-start = (bf16[3,6,1024]{2,1,0:T(8,128)(2,1)S(1)}, bf16[3,6,1024]{2,1,0:T(8,128)(2,1)S(1)}, u32[]{:S(2)}, u32[]{:S(2)}) collective-permute-start(bf16[3,6,1024]{2,1,0:T(8,128)(2,1)S(1)} %slice.89), channel_id=1, source_target_pairs={{0,8},{8,16},{16,24},{24,32},{32,40},{40,48},{48,56},{56,64},{64,7... | collective-permute-start | bytes 110600 | tf_op jit(solution)/shard_map/ppermute | solution.py:17
  7.3 13.2 %multiply_add_fusion = f32[3,512,1024]{2,1,0:T(8,128)S(1)} fusion(bf16[3,512,1024]{2,1,0:T(8,128)(2,1)} %param.5, bf16[3,6,1024]{2,1,0:T(8,128)(2,1)S(1)} %collective-permute-done, f32[3,1024]{1,0:T(4,128)S(1)} %get-tuple-element.32, f32[3,1024]{1,0:T(4,128)S(1)} %get-tuple-element.33, f32[3,1024]{1,0:T(4,128)S(1)} %get-tuple-element.34, ...), kind=kLoop, calls=%fused_computation.6 | loop fusion | flops 59768832 | bytes 9560064 | tf_op jit(solution)/shard_map/add | solution.py:45
  21.3 3.5 copy.70
  24.8 13.1 %all-to-all-start = ((bf16[2,1,512,1024]{3,0,1,2:T(2,128)(2,1)}), bf16[2,1,512,1024]{3,0,1,2:T(2,128)(2,1)S(1)}, u32[]{:S(2)}, u32[]{:S(2)}) async-start(bf16[2,1,512,1024]{3,0,1,2:T(2,128)(2,1)} %copy.70), calls=%async_computation | async-start | bytes 4194304 | tf_op jit(solution)/shard_map/all_to_all | solution.py:63
  38.0 50.7 %all-to-all-done = bf16[2,1,512,1024]{3,0,1,2:T(2,128)(2,1)S(1)} async-done(((bf16[2,1,512,1024]{3,0,1,2:T(2,128)(2,1)}), bf16[2,1,512,1024]{3,0,1,2:T(2,128)(2,1)S(1)}, u32[]{:S(2)}, u32[]{:S(2)}) %all-to-all-start) | async-done | bytes 2097184 | tf_op jit(solution)/shard_map/all_to_all | solution.py:63
  88.7 3.9 fusion.120
  97.6 4.3 copy.76
  102.0 6.0 %all-to-all-start.1 = ((bf16[2,64,16,1024]{3,2,0,1:T(8,128)(2,1)}), bf16[2,64,16,1024]{3,2,0,1:T(8,128)(2,1)}, u32[]{:S(2)}, u32[]{:S(2)}) async-start(bf16[2,64,16,1024]{3,2,0,1:T(8,128)(2,1)} %copy.76), calls=%async_computation.1 | async-start | bytes 8388608 | tf_op jit(solution)/shard_map/all_to_all | solution.py:82
  108.0 4.7 fusion.118
  115.6 4.0 copy.104
  119.7 84.4 %all-to-all-done.1 = bf16[2,64,16,1024]{3,2,0,1:T(8,128)(2,1)} async-done(((bf16[2,64,16,1024]{3,2,0,1:T(8,128)(2,1)}), bf16[2,64,16,1024]{3,2,0,1:T(8,128)(2,1)}, u32[]{:S(2)}, u32[]{:S(2)}) %all-to-all-start.1) | async-done | bytes 4194336 | tf_op jit(solution)/shard_map/all_to_all | solution.py:82
  207.8 8.8 %fusion.37 = f32[2,1024,512]{2,1,0:T(8,128)S(1)} fusion(bf16[2,512,1024]{2,1,0:T(8,128)(2,1)S(1)} %bitcast.110), kind=kOutput, calls=%fused_computation.68 | convolution fusion | flops 1077673984 | bytes 6291456 | tf_op jit(solution)/shard_map/jm,kmc->kjc/dot_general | solution.py:83
  216.8 8.8 %fusion.35 = f32[2,1024,512]{2,1,0:T(8,128)S(1)} fusion(bf16[2,512,1024]{2,1,0:T(8,128)(2,1)S(1)} %bitcast.112), kind=kOutput, calls=%fused_computation.67 | convolution fusion | flops 1077673984 | bytes 6291456 | tf_op jit(solution)/shard_map/jm,kmc->kjc/dot_general | solution.py:86
  225.6 10.5 %convolution_subtract_fusion.1 = f32[2,1024,512]{2,1,0:T(8,128)S(1)} fusion(f32[2,1024,512]{2,1,0:T(8,128)S(1)} %fusion.37, bf16[2,512,1024]{2,1,0:T(8,128)(2,1)S(1)} %bitcast.113), kind=kOutput, calls=%fused_computation.33 | convolution fusion | flops 1078722560 | bytes 10485760 | tf_op jit(solution)/shard_map/jm,kmc->kjc/dot_general | solution.py:85
  236.1 7.3 %fusion.3 = (bf16[2,512,1024]{1,2,0:T(8,128)(2,1)S(1)}, bf16[2,512,1024]{1,2,0:T(8,128)(2,1)S(1)}) fusion(f32[2,1024,512]{2,1,0:T(8,128)S(1)} %convolution_subtract_fusion.1, bf16[1,2,512,1024]{2,3,1,0:T(8,128)(2,1)S(1)} %copy.106, bf16[1,2,512,1024]{2,3,1,0:T(8,128)(2,1)S(1)} %copy-done, f32[2,1024,512]{2,1,0:T(8,128)S(1)} %fusion.35, ...), kind=kOutput, calls=%fused_computation.14 | convolution fusion | flops 1089208320 | bytes 18874368 | tf_op jit(solution)/shard_map/jm,kmc->kjc/dot_general | solution.py:88
  243.3 7.3 %fusion.31 = f32[2,1024,512]{2,1,0:T(8,128)S(1)} fusion(bf16[2,512,1024]{1,2,0:T(8,128)(2,1)S(1)} %get-tuple-element.5), kind=kOutput, calls=%fused_computation.65 | convolution fusion | flops 1077673984 | bytes 6291456 | tf_op jit(solution)/shard_map/jm,kjc->kmc/dot_general | solution.py:94
  250.6 7.3 %fusion.33 = f32[2,1024,512]{2,1,0:T(8,128)S(1)} fusion(bf16[2,512,1024]{1,2,0:T(8,128)(2,1)S(1)} %get-tuple-element.6), kind=kOutput, calls=%fused_computation.66 | convolution fusion | flops 1077673984 | bytes 6291456 | tf_op jit(solution)/shard_map/jm,kjc->kmc/dot_general | solution.py:91
  257.9 8.2 %convolution_subtract_fusion = f32[2,1024,512]{2,1,0:T(8,128)S(1)} fusion(f32[2,1024,512]{2,1,0:T(8,128)S(1)} %fusion.31, bf16[2,512,1024]{1,2,0:T(8,128)(2,1)S(1)} %get-tuple-element.6), kind=kOutput, calls=%fused_computation.30 | convolution fusion | flops 1078722560 | bytes 10485760 | tf_op jit(solution)/shard_map/jm,kjc->kmc/dot_general | solution.py:96
  266.1 6.7 %fusion.11 = (bf16[1,2,512,1024]{2,3,1,0:T(8,128)(2,1)S(1)}, bf16[1,2,512,1024]{2,3,1,0:T(8,128)(2,1)S(1)}) fusion(f32[2,1024,512]{2,1,0:T(8,128)S(1)} %convolution_subtract_fusion, f32[2,512]{1,0:T(2,128)S(1)} %get-tuple-element.27, f32[2,512]{1,0:T(2,128)S(1)} %get-tuple-element.26, f32[2,1024,512]{2,1,0:T(8,128)S(1)} %fusion.33, ...), kind=kOutput, calls=%fused_computation.36 | convolution fusion | flops 1087111168 | bytes 14688256 | tf_op jit(solution)/shard_map/jm,kjc->kmc/dot_general | solution.py:93
  275.2 11.3 %copy.85 = bf16[2,2,512,1024]{3,1,0,2:T(2,128)(2,1)} copy(bf16[2,2,512,1024]{2,3,1,0:T(8,128)(2,1)} %pad_maximum_fusion.1) | data formatting | bytes 8388608 | tf_op jit(solution)/shard_map/stack | solution.py:103
  286.5 7.7 %all-to-all-start.2 = ((bf16[2,2,512,1024]{3,1,0,2:T(2,128)(2,1)}), bf16[2,2,512,1024]{3,1,0,2:T(2,128)(2,1)}, u32[]{:S(2)}, u32[]{:S(2)}) async-start(bf16[2,2,512,1024]{3,1,0,2:T(2,128)(2,1)} %copy.85), calls=%async_computation.2 | async-start | bytes 8388608 | tf_op jit(solution)/shard_map/all_to_all | solution.py:109
  295.0 95.3 %all-to-all-done.2 = bf16[2,2,512,1024]{3,1,0,2:T(2,128)(2,1)} async-done(((bf16[2,2,512,1024]{3,1,0,2:T(2,128)(2,1)}), bf16[2,2,512,1024]{3,1,0,2:T(2,128)(2,1)}, u32[]{:S(2)}, u32[]{:S(2)}) %all-to-all-start.2) | async-done | bytes 4194336 | tf_op jit(solution)/shard_map/all_to_all | solution.py:109
  390.3 3.5 copy.86
  395.8 3.5 copy.87
  399.3 4.1 squeeze.13
  403.4 3.5 fusion.52
  406.9 3.5 copy.88
  410.4 4.1 squeeze.14
  414.6 6.3 %multiply_reduce_fusion = (f32[32,16]{0,1:T(8,128)S(1)}, f32[32,16,1024]{2,0,1:T(8,128)}) fusion(bf16[32,16,1024]{2,1,0:T(8,128)(2,1)S(1)} %bitcast.107, f32[1024]{0:T(1024)S(1)} %copy-done.3, f32[32,16,1024]{2,0,1:T(8,128)} %fusion.52, bf16[64,16,1024]{2,0,1:T(8,128)(2,1)} %squeeze.14, f32[32,16,1024]{2,1,0:T(8,128)S(1)} %convert.9), kind=kOutput, calls=%fused_computation.44 | convolution fusion | flops 71333376 | bytes 9443328 | tf_op jit(solution)/shard_map/nk,kmc->nmc/dot_general | solution.py:112
  420.9 15.3 %psum.7 = f32[32,16]{0,1:T(8,128)S(1)} all-reduce(f32[32,16]{0,1:T(8,128)S(1)} %get-tuple-element.30), channel_id=1, replica_groups=mesh['seq'=32,'chan'=8] {'chan'}, use_global_device_ids=true, to_apply=%region_1.2 | all-reduce | flops 512 | bytes 4096 | tf_op jit(solution)/shard_map/psum | solution.py:115
  440.4 11.6 %all-to-all-start.3 = ((bf16[32,16,1024]{2,1,0:T(8,128)(2,1)}), bf16[32,16,1024]{2,1,0:T(8,128)(2,1)S(1)}, u32[]{:S(2)}, u32[]{:S(2)}) async-start(bf16[32,16,1024]{2,1,0:T(8,128)(2,1)} %broadcast_select_fusion), calls=%async_computation.3 | async-start | bytes 2097152 | tf_op jit(solution)/shard_map/all_to_all | solution.py:124
  451.9 27.7 %all-to-all-done.3 = bf16[32,16,1024]{2,1,0:T(8,128)(2,1)S(1)} async-done(((bf16[32,16,1024]{2,1,0:T(8,128)(2,1)}), bf16[32,16,1024]{2,1,0:T(8,128)(2,1)S(1)}, u32[]{:S(2)}, u32[]{:S(2)}) %all-to-all-start.3) | async-done | bytes 1048608 | tf_op jit(solution)/shard_map/all_to_all | solution.py:124
  (46 shorter events, 25.4 us)
Async XLA Ops:
  0.8 6.5 %collective-permute-start = (bf16[3,6,1024]{2,1,0:T(8,128)(2,1)S(1)}, bf16[3,6,1024]{2,1,0:T(8,128)(2,1)S(1)}, u32[]{:S(2)}, u32[]{:S(2)}) collective-permute-start(bf16[3,6,1024]{2,1,0:T(8,128)(2,1)S(1)} %slice.89), channel_id=1, source_target_pairs={{0,8},{8,16},{16,24},{24,32},{32,40},{40,48},{48,56},{56,64},{64,7... | collective-permute-start | bytes 110600 | tf_op jit(solution)/shard_map/ppermute | solution.py:17
  24.8 64.0 %all-to-all-start = ((bf16[2,1,512,1024]{3,0,1,2:T(2,128)(2,1)}), bf16[2,1,512,1024]{3,0,1,2:T(2,128)(2,1)S(1)}, u32[]{:S(2)}, u32[]{:S(2)}) async-start(bf16[2,1,512,1024]{3,0,1,2:T(2,128)(2,1)} %copy.70), calls=%async_computation | async-start | bytes 4194304 | tf_op jit(solution)/shard_map/all_to_all | solution.py:63
  102.0 102.2 %all-to-all-start.1 = ((bf16[2,64,16,1024]{3,2,0,1:T(8,128)(2,1)}), bf16[2,64,16,1024]{3,2,0,1:T(8,128)(2,1)}, u32[]{:S(2)}, u32[]{:S(2)}) async-start(bf16[2,64,16,1024]{3,2,0,1:T(8,128)(2,1)} %copy.76), calls=%async_computation.1 | async-start | bytes 8388608 | tf_op jit(solution)/shard_map/all_to_all | solution.py:82
  225.6 10.5 %copy-start = (bf16[1,2,512,1024]{2,3,1,0:T(8,128)(2,1)S(1)}, bf16[1,2,512,1024]{2,3,1,0:T(8,128)(2,1)}, u32[]{:S(2)}) copy-start(bf16[1,2,512,1024]{2,3,1,0:T(8,128)(2,1)} %copy.104) | copy-start | bytes 6291460
  286.5 7.8 %copy-start.1 = (bf16[1,1,512,1024]{3,0,1,2:T(2,128)(2,1)S(1)}, bf16[1,1,512,1024]{3,0,1,2:T(2,128)(2,1)}, u32[]{:S(2)}) copy-start(bf16[1,1,512,1024]{3,0,1,2:T(2,128)(2,1)} %get-tuple-element.18) | copy-start | bytes 3145732
  286.5 103.7 %all-to-all-start.2 = ((bf16[2,2,512,1024]{3,1,0,2:T(2,128)(2,1)}), bf16[2,2,512,1024]{3,1,0,2:T(2,128)(2,1)}, u32[]{:S(2)}, u32[]{:S(2)}) async-start(bf16[2,2,512,1024]{3,1,0,2:T(2,128)(2,1)} %copy.85), calls=%async_computation.2 | async-start | bytes 8388608 | tf_op jit(solution)/shard_map/all_to_all | solution.py:109
  403.4 3.5 copy-start.2
  406.9 7.6 %copy-start.3 = (f32[1024]{0:T(1024)S(1)}, f32[1024]{0:T(1024)}, u32[]{:S(2)}) copy-start(f32[1024]{0:T(1024)} %param.8) | copy-start | bytes 12292
  414.6 21.6 %copy-start.4 = (f32[1024]{0:T(1024)S(1)}, f32[1024]{0:T(1024)}, u32[]{:S(2)}) copy-start(f32[1024]{0:T(1024)} %param.9) | copy-start | bytes 12292
  440.4 39.3 %all-to-all-start.3 = ((bf16[32,16,1024]{2,1,0:T(8,128)(2,1)}), bf16[32,16,1024]{2,1,0:T(8,128)(2,1)S(1)}, u32[]{:S(2)}, u32[]{:S(2)}) async-start(bf16[32,16,1024]{2,1,0:T(8,128)(2,1)} %broadcast_select_fusion), calls=%async_computation.3 | async-start | bytes 2097152 | tf_op jit(solution)/shard_map/all_to_all | solution.py:124
where the time goes:
time: 488 us; the launch traced here: 481 us
  waiting for transfers between devices  258 us (53%)
  matrix products  78.9 us (16%)
  local copies, waits for them, and re-layouts  63.6 us (13%)
  starting transfers between devices  43.4 us (9%)
  other arithmetic  21.3 us (4%)
  blocking collectives  15.3 us (3%)
    all_to_all x1, waiting for transfers between devices, body(): lax.all_to_all(returned, 'seq', split_axis=2, concat_axis=1, tiled=True)  95.3 us
    all_to_all x1, waiting for transfers between devices, body(): lax.all_to_all(first, 'seq', split_axis=1, concat_axis=2, tiled=True)  84.4 us
    all_to_all x1, waiting for transfers between devices, body(): lax.all_to_all(jnp.stack([gated, gate])[:, None], 'seq', split_axis=2, co...  50.7 us
    all_to_all x1, waiting for transfers between devices, body(): lax.all_to_all(jnp.take(normed, order, axis=0), 'seq', split_axis=0, conc...  27.7 us
    psum x1, blocking collectives, body(): power = lax.psum(jnp.sum(mixed * mixed, axis=-1), 'chan') / D  15.3 us
    add x1, other arithmetic, short_filters(): shorts + short_weight[:, tap_index, None, :] * extended[:, offset:offset...  13.2 us
    all_to_all x1, starting transfers between devices, body(): lax.all_to_all(jnp.stack([gated, gate])[:, None], 'seq', split_axis=2, co...  13.1 us
    all_to_all x1, starting transfers between devices, body(): lax.all_to_all(jnp.take(normed, order, axis=0), 'seq', split_axis=0, conc...  11.6 us
  transfers between devices with their start and end apart: 5, of which 4 were waited for; matrix products, arithmetic and copies ran while one was open for 3% of the time, Pallas kernels for 0%

commit v1 on v0

v1 whole, which is shorter than its diff:
```python
import functools
import math

import jax
import jax.numpy as jnp
import ml_dtypes
import numpy as np
from jax import lax
from jax.experimental import pallas as pl
from jax.experimental.pallas import tpu as pltpu
from jax.sharding import PartitionSpec as P

MESH = pl.DeviceIdType.MESH
F32 = jnp.float32
BF16 = jnp.bfloat16

D = 8192
EPSILON = 1e-05
LENGTH = 16384
SHARDS = 32
CHANS = 8
ROWS = 512
WIDTH = 1024
OWN = 32
GROUP = 16
HALO = 16
TAPS = 7


def turn(numerator, period):
    angle = np.asarray(numerator % period, np.float64) * (2.0 * math.pi / period)
    return np.cos(angle), np.sin(angle)


@functools.cache
def tables():
    outer = np.arange(SHARDS)
    inner = np.arange(ROWS)
    eye = np.eye(GROUP)
    cos_k, sin_k = turn(np.outer(np.arange(256), inner), ROWS)
    spectrum_in = np.block([[cos_k, sin_k], [-sin_k, cos_k]])
    cos_f, sin_f = turn(np.outer(inner, inner), ROWS)
    forward = np.block([[cos_f, -sin_f], [sin_f, cos_f]])
    inverse = np.block([[cos_f, sin_f], [-sin_f, cos_f]])
    cos_s, sin_s = turn(np.outer(2 * outer + 1, outer), 64)
    cos_a, sin_a = turn(np.outer(4 * outer + 1, outer), 128)
    scale = 2.0 / LENGTH
    filter_outer = scale * np.block(
        [[cos_a @ cos_s.T, -cos_a @ sin_s.T], [-sin_a @ cos_s.T, sin_a @ sin_s.T]]
    )
    outer_in = np.concatenate([cos_a, -sin_a], axis=0)
    outer_out = np.concatenate([cos_a.T, -sin_a.T], axis=1) / LENGTH
    filter_turn = turn(np.outer(2 * outer + 1, inner), 2 * LENGTH)
    value_turn = turn(np.outer(4 * outer + 1, inner), 4 * LENGTH)
    value_turn = (value_turn[0], -value_turn[1])
    matrices = (
        spectrum_in,
        np.kron(filter_outer, eye),
        forward,
        np.kron(outer_in, eye),
        inverse,
        np.kron(outer_out, eye),
    )
    turns = [np.broadcast_to(t[:, None, :], (SHARDS, 8, ROWS)) for t in (*filter_turn, *value_turn)]
    return tuple(m.astype(ml_dtypes.bfloat16) for m in matrices) + tuple(
        np.ascontiguousarray(t, np.float32) for t in turns
    )


def dot(left, right):
    return jnp.dot(left, right, preferred_element_type=F32)


def rows_of(value):
    return value.reshape(SHARDS, 2, 8, value.shape[-1])


def kernel(
    proj,
    spectrum,
    weight,
    skip,
    gain,
    h_spectrum_in,
    h_filter_outer,
    h_forward,
    h_outer_in,
    h_inverse,
    h_outer_out,
    h_filter_cos,
    h_filter_sin,
    h_value_cos,
    h_value_sin,
    out,
    spec_local,
    proj_local,
    spec_send,
    gated_send,
    gate_send,
    spec_got,
    gated_got,
    gate_got,
    mixed_send,
    mixed_got,
    spectrum_in,
    filter_outer,
    forward,
    outer_in,
    inverse,
    outer_out,
    filter_cos,
    filter_sin,
    value_cos,
    value_sin,
    filter_freq,
    stacked_rows,
    stacked_lanes,
    unmixed,
    skip_own,
    power_send,
    power_got,
    load_sem,
    table_sem,
    halo_sem,
    send_sem,
    got_sem,
    power_send_sem,
    power_got_sem,
):
    me = lax.axis_index("seq")
    my_chan = lax.axis_index("chan")

    spec_load = pltpu.make_async_copy(spectrum.at[:, 1, pl.ds(0, 256), :], spec_local, load_sem.at[0])
    proj_load = pltpu.make_async_copy(proj, proj_local.at[:, pl.ds(HALO, ROWS), :], load_sem.at[1])
    spec_load.start()
    proj_load.start()
    loads = [
        pltpu.make_async_copy(source, target, table_sem.at[index])
        for index, (source, target) in enumerate(
            (
                (h_spectrum_in, spectrum_in),
                (h_filter_outer, filter_outer),
                (h_forward, forward),
                (h_outer_in, outer_in),
                (h_inverse, inverse),
                (h_outer_out, outer_out),
                (h_filter_cos, filter_cos),
                (h_filter_sin, filter_sin),
                (h_value_cos, value_cos),
                (h_value_sin, value_sin),
            )
        )
    ]
    for load in loads:
        load.start()

    barrier = pltpu.get_barrier_semaphore()

    @pl.loop(1, SHARDS)
    def _(k):
        pl.semaphore_signal(
            barrier, inc=1, device_id={"seq": lax.rem(me + k, SHARDS)}, device_id_type=MESH
        )

    @pl.loop(1, CHANS)
    def _(k):
        pl.semaphore_signal(
            barrier, inc=1, device_id={"chan": lax.rem(my_chan + k, CHANS)}, device_id_type=MESH
        )

    column = pl.multiple_of((me // 4) * 128, 128)
    wide = jnp.transpose(jnp.broadcast_to(skip[:, pl.ds(column, 128)], (128, 128)))
    unmixed[0, pl.ds(0, 128), pl.ds(0, 128)] = wide
    mine = unmixed[0, pl.ds(pl.multiple_of(lax.rem(me, 4) * OWN, OWN), OWN), pl.ds(0, 128)]
    skip_own[:, pl.ds(0, 128)] = mine
    skip_own[:, pl.ds(128, 128)] = mine

    pl.semaphore_wait(barrier, SHARDS - 1 + CHANS - 1)

    halo = pltpu.make_async_remote_copy(
        src_ref=proj.at[:, pl.ds(ROWS - HALO, HALO), :],
        dst_ref=proj_local.at[:, pl.ds(0, HALO), :],
        send_sem=halo_sem.at[0],
        recv_sem=halo_sem.at[1],
        device_id={"seq": lax.rem(me + 1, SHARDS)},
        device_id_type=MESH,
    )

    @pl.when(me < SHARDS - 1)
    def _():
        halo.start()

    def own_rows(device):
        return pl.ds(pl.multiple_of(device * OWN, OWN), OWN)

    def send_all(source, target, which):
        @pl.loop(1, SHARDS)
        def _(k):
            device = lax.rem(me + k, SHARDS)
            pltpu.make_async_remote_copy(
                src_ref=source.at[device],
                dst_ref=target.at[me],
                send_sem=send_sem.at[which],
                recv_sem=got_sem.at[which],
                device_id={"seq": device},
                device_id_type=MESH,
            ).start()

        target[me] = source[me]

    def wait_all(ref, sem):
        part = ref.at[pl.ds(0, SHARDS - 1)]
        pltpu.make_async_copy(part, part, sem).wait()

    spec_load.wait()

    @pl.loop(0, WIDTH // 128)
    def _(block):
        columns = pl.ds(pl.multiple_of(block * 128, 128), 128)
        for part in range(2):
            value = jnp.transpose(spec_local[part, :, columns].astype(F32)).astype(BF16)
            spec_send[pl.ds(block * 4, 4), :, pl.ds(part * 256, 256)] = value.reshape(4, OWN, 256)

    send_all(spec_send, spec_got, 0)

    proj_load.wait()

    @pl.when(me == 0)
    def _():
        proj_local[:, pl.ds(0, HALO), :] = jnp.zeros((3, HALO, WIDTH), BF16)

    @pl.when(me > 0)
    def _():
        halo.wait_recv()

    @pl.loop(0, WIDTH // 128)
    def _(block):
        columns = pl.ds(pl.multiple_of(block * 128, 128), 128)

        @pl.loop(0, ROWS // 128)
        def _(tile):
            start = pl.multiple_of(tile * 128, 128)
            shorts = []
            for feature in range(3):
                taken = proj_local[feature, pl.ds(start, 128 + HALO), columns].astype(F32)
                total = jnp.zeros((128, 128), F32)
                for tap in range(TAPS):
                    total = (
                        total
                        + weight[feature, pl.ds(tap, 1), columns] * taken[HALO - tap : HALO - tap + 128]
                    )
                shorts.append(total)
            places = pl.ds(start, 128)
            gate_send[pl.ds(block * 4, 4), :, places] = (
                jnp.transpose(shorts[0]).astype(BF16).reshape(4, OWN, 128)
            )
            gated_send[pl.ds(block * 4, 4), :, places] = (
                jnp.transpose(shorts[1] * shorts[2]).astype(BF16).reshape(4, OWN, 128)
            )

    send_all(gated_send, gated_got, 1)

    for load in loads:
        load.wait()
    wait_all(spec_got, got_sem.at[0])

    def turned(real, imag, cosine, sine, lanes, sign):
        real, imag = rows_of(real), rows_of(imag)
        c = cosine[:, :, lanes].reshape(SHARDS, 1, 8, 256)
        s = sine[:, :, lanes].reshape(SHARDS, 1, 8, 256)
        if sign > 0:
            new = (c * real - s * imag, c * imag + s * real)
        else:
            new = (c * real + s * imag, c * imag - s * real)
        return tuple(v.reshape(ROWS, 256).astype(BF16) for v in new)

    halves = (pl.ds(0, 256), pl.ds(256, 256))
    uppers = (pl.ds(512, 256), pl.ds(768, 256))
    top, bottom = pl.ds(0, ROWS), pl.ds(ROWS, ROWS)

    @pl.loop(0, OWN // GROUP)
    def _(group):
        chans = pl.ds(pl.multiple_of(group * GROUP, GROUP), GROUP)
        taken = spec_got[:, chans, :].reshape(ROWS, ROWS)
        for low, high in zip(halves, uppers):
            real, imag = dot(taken, spectrum_in[:, low]), dot(taken, spectrum_in[:, high])
            real, imag = turned(real, imag, filter_cos, filter_sin, low, 1)
            stacked_rows[top, low] = real
            stacked_rows[bottom, low] = imag
        for low, high in zip(halves, uppers):
            both = dot(filter_outer[...], stacked_rows[:, low])
            real, imag = turned(both[:ROWS], both[ROWS:], value_cos, value_sin, low, 1)
            stacked_lanes[:, low] = real
            stacked_lanes[:, high] = imag
        for lanes in (*halves, *uppers):
            filter_freq[group, :, lanes] = dot(stacked_lanes[...], forward[:, lanes])

    wait_all(gated_got, got_sem.at[1])
    send_all(gate_send, gate_got, 2)

    @pl.loop(0, OWN // GROUP)
    def _(group):
        chans = pl.ds(pl.multiple_of(group * GROUP, GROUP), GROUP)
        for low, high in zip(halves, uppers):
            both = dot(outer_in[...], gated_got[:, chans, low].reshape(ROWS, 256))
            real, imag = turned(both[:ROWS], both[ROWS:], value_cos, value_sin, low, 1)
            stacked_lanes[:, low] = real
            stacked_lanes[:, high] = imag
        for low, high in zip(halves, uppers):
            real, imag = dot(stacked_lanes[...], forward[:, low]), dot(stacked_lanes[...], forward[:, high])
            f_real, f_imag = filter_freq[group, :, low], filter_freq[group, :, high]
            stacked_rows[top, low] = (f_real * real - f_imag * imag).astype(BF16)
            stacked_rows[bottom, low] = (f_real * imag + f_imag * real).astype(BF16)
        for low, high in zip(halves, uppers):
            real = dot(stacked_rows[top, :], inverse[top, low]) + dot(
                stacked_rows[bottom, :], inverse[bottom, low]
            )
            imag = dot(stacked_rows[top, :], inverse[top, high]) + dot(
                stacked_rows[bottom, :], inverse[bottom, high]
            )
            real, imag = turned(real, imag, value_cos, value_sin, low, -1)
            stacked_lanes[:, low] = real
            stacked_lanes[:, high] = imag
        for low, high in zip(halves, uppers):
            value = dot(outer_out[:, top], stacked_lanes[:, low]) + dot(
                outer_out[:, bottom], stacked_lanes[:, high]
            )
            own = gated_got[:, chans, low].astype(F32)
            unmixed[group, :, low] = (
                value.reshape(SHARDS, GROUP, 256) + skip_own[chans, :][None] * own
            ).reshape(ROWS, 256)

    wait_all(gate_got, got_sem.at[2])

    for side in range(2):

        @pl.loop(0, OWN // GROUP)
        def _(group):
            chans = pl.ds(pl.multiple_of(group * GROUP, GROUP), GROUP)
            for half, lanes in enumerate(halves):
                value = unmixed[group, pl.ds(side * 256, 256), lanes].reshape(16, GROUP, 256)
                value = (gate_got[pl.ds(side * 16, 16), chans, lanes].astype(F32) * value).astype(BF16)
                for index in range(16):
                    device = 2 * index + half if side == 0 else 31 - 2 * index - half
                    mixed_send[side, device, chans, :] = value[index]

        send_all(mixed_send.at[side], mixed_got.at[side], 3 + side)

    for side in range(2):
        wait_all(mixed_got.at[side], got_sem.at[3 + side])

        def squares(block, total):
            value = mixed_got[side, pl.ds(block * 4, 4), :, :].astype(F32)
            value = (value * value).reshape(16, 8, 256)
            return total + jnp.sum(value, axis=0)

        power = lax.fori_loop(0, WIDTH // 128, squares, jnp.zeros((8, 256), F32))
        power_send[side] = power
        power_got[side, my_chan] = power

        @pl.loop(1, CHANS)
        def _(k):
            pltpu.make_async_remote_copy(
                src_ref=power_send.at[side],
                dst_ref=power_got.at[side, my_chan],
                send_sem=power_send_sem.at[side],
                recv_sem=power_got_sem.at[side],
                device_id={"chan": lax.rem(my_chan + k, CHANS)},
                device_id_type=MESH,
            ).start()

        @pl.loop(0, WIDTH // 128)
        def _(block):
            value = mixed_got[side, pl.ds(block * 4, 4), :, :].reshape(128, 256).astype(F32)
            columns = pl.ds(pl.multiple_of(block * 128, 128), 128)
            out[pl.ds(side * 256, 256), columns] = jnp.transpose(value).astype(BF16)

    for side in range(2):
        part = power_got.at[side, pl.ds(0, CHANS - 1)]
        pltpu.make_async_copy(part, part, power_got_sem.at[side]).wait()
        power = jnp.sum(jnp.sum(power_got[side], axis=0), axis=0, keepdims=True)
        scale = lax.rsqrt(power * (1.0 / D) + EPSILON)
        scale = jnp.transpose(jnp.broadcast_to(scale, (128, 256)))

        @pl.loop(0, WIDTH // 128)
        def _(block):
            columns = pl.ds(pl.multiple_of(block * 128, 128), 128)
            rows = pl.ds(side * 256, 256)
            out[rows, columns] = (out[rows, columns].astype(F32) * scale * gain[:, columns]).astype(BF16)

    @pl.when(me < SHARDS - 1)
    def _():
        halo.wait_send()

    wait_all(spec_send, send_sem.at[0])
    wait_all(gated_send, send_sem.at[1])
    wait_all(gate_send, send_sem.at[2])
    for side in range(2):
        wait_all(mixed_send.at[side], send_sem.at[3 + side])
        part = power_got.at[side, pl.ds(0, CHANS - 1)]
        pltpu.make_async_copy(part, part, power_send_sem.at[side]).wait()


def body(proj, short_weight, spectrum, skip, gain):
    constants = tables()
    held = [pltpu.VMEM(c.shape, c.dtype) for c in constants]
    whole = (SHARDS, OWN, ROWS)
    anywhere = pl.BlockSpec(memory_space=pl.ANY)
    inside = pl.BlockSpec(memory_space=pltpu.VMEM)
    value = pl.pallas_call(
        kernel,
        out_shape=jax.ShapeDtypeStruct((ROWS, WIDTH), BF16),
        in_specs=[anywhere, anywhere, inside, inside, inside] + [anywhere] * len(constants),
        out_specs=inside,
        scratch_shapes=[
            pltpu.VMEM((2, 256, WIDTH), BF16),
            pltpu.VMEM((3, HALO + ROWS, WIDTH), BF16),
            pltpu.VMEM(whole, BF16),
            pltpu.VMEM(whole, BF16),
            pltpu.VMEM(whole, BF16),
            pltpu.VMEM(whole, BF16),
            pltpu.VMEM(whole, BF16),
            pltpu.VMEM(whole, BF16),
            pltpu.VMEM((2, SHARDS, OWN, 256), BF16),
            pltpu.VMEM((2, SHARDS, OWN, 256), BF16),
            *held,
            pltpu.VMEM((OWN // GROUP, ROWS, 2 * ROWS), F32),
            pltpu.VMEM((2 * ROWS, ROWS), BF16),
            pltpu.VMEM((ROWS, 2 * ROWS), BF16),
            pltpu.VMEM((OWN // GROUP, ROWS, ROWS), F32),
            pltpu.VMEM((OWN, 256), F32),
            pltpu.VMEM((2, 8, 256), F32),
            pltpu.VMEM((2, CHANS, 8, 256), F32),
            pltpu.SemaphoreType.DMA((2,)),
            pltpu.SemaphoreType.DMA((len(constants),)),
            pltpu.SemaphoreType.DMA((2,)),
            pltpu.SemaphoreType.DMA((5,)),
            pltpu.SemaphoreType.DMA((5,)),
            pltpu.SemaphoreType.DMA((2,)),
            pltpu.SemaphoreType.DMA((2,)),
        ],
        compiler_params=pltpu.CompilerParams(
            collective_id=0, has_side_effects=True, vmem_limit_bytes=56 * 2**20
        ),
    )(proj, spectrum, short_weight, skip[None], gain[None], *(jnp.asarray(c) for c in constants))
    return value.reshape(1, 2, ROWS // 2, WIDTH)


def solution(mesh):
    placed = (
        P(None, "seq", "chan"),
        P(None, None, "chan"),
        P(None, "seq", None, "chan"),
        P("chan"),
        P("chan"),
    )
    return jax.shard_map(
        body, mesh=mesh, in_specs=placed, out_specs=P("seq", None, None, "chan"), check_vma=False
    )
```

time: 488 us -> 122 us (0.25); the launches traced: 481 us -> 122 us
  waiting for transfers between devices: 258 us -> 0 us
  Pallas kernels: 0 us -> 119 us
  matrix products: 78.9 us -> 0 us
  local copies, waits for them, and re-layouts: 63.6 us -> 2.26 us
  starting transfers between devices: 43.4 us -> 0 us
  other arithmetic: 21.3 us -> 0 us
  blocking collectives: 15.3 us -> 0 us
    all_to_all x4 -> x0, waiting for transfers between devices: 258 us -> none  [the longest x1 95.3 us: body(): lax.all_to_all(returned, 'seq', split_axis=2, concat_axis=1, tiled=True)]
    pallas_call x0 -> x1, Pallas kernels: none -> 119 us  [body(): pl.pallas_call(kernel, out_shape=jax.ShapeDtypeStruct((ROWS, WIDTH), BF16...]
    dot_general x12 -> x0, matrix products: 78.9 us -> none  [the longest x1 10.5 us: body(): jnp.einsum('jm,kmc->kjc', inner_sin, spectral[1], preferred_element_type=...]
    all_to_all x4 -> x0, starting transfers between devices: 38.5 us -> none  [the longest x1 13.1 us: body(): lax.all_to_all(jnp.stack([gated, gate])[:, None], 'seq', split_axis=2, co...]
    slice x11 -> x0, local copies, waits for them, and re-layouts: 21.2 us -> none  [the longest x2 5.46 us: body(): columns_back[1]]
    another operation x2 -> x0, local copies, waits for them, and re-layouts: 15.7 us -> none  [the longest x1 11.3 us: body(): jnp.stack([(return_cos * spread_re + return_sin * spread_im).astype(jnp.b...]
    psum x1 -> x0, blocking collectives: 15.3 us -> none  [body(): power = lax.psum(jnp.sum(mixed * mixed, axis=-1), 'chan') / D]
    add x3 -> x0, other arithmetic: 13.2 us -> none  [the longest x1 13.2 us: short_filters(): shorts + short_weight[:, tap_index, None, :] * extended[:, offset:offset...]
  transfers between devices with their start and end apart: 5 -> 0, of which waited for: 4 -> 0; matrix products, arithmetic and copies ran while one was open for 3% -> 0% of each run, Pallas kernels for 0% -> 0%
where the time goes in v1:
time: 122 us
  Pallas kernels  119 us (98%)
  local copies, waits for them, and re-layouts  2.26 us (2%)
    pallas_call x1, Pallas kernels, body(): pl.pallas_call(kernel, out_shape=jax.ShapeDtypeStruct((ROWS, WIDTH), BF16...  119 us

profile of v1, /device:TPU:1, one launch (start us, length us, event | category | flops | bytes accessed | tf_op | source)
XLA Modules:
  0.0 121.6 jit_solution(2053501384063654992)
XLA Ops:
  0.0 119.3 %shard_map.145 = bf16[512,1024]{1,0:T(8,128)(2,1)} custom-call(bf16[3,512,1024]{2,1,0:T(8,128)(2,1)} %proj.1, bf16[2,2,512,1024]{3,2,1,0:T(8,128)(2,1)} %spectrum.1, f32[3,7,1024]{2,1,0:T(8,128)} %weight.1, f32[1,1024]{1,0:T(1,128)} %bitcast.4, f32[1,1024]{1,0:T(1,128)} %bitcast.5, bf16[512,1024]{1,0:T(8,128)(2,1)} %constant.20.clone.h_spectrum_in, ...), custom_call_target="tpu_custom_call" | custom-call | tf_op jit(solution)/shard_map/pallas_call | solution.py:410
  119.3 2.3 %copy.17 = bf16[1,2,256,1024]{3,2,1,0:T(8,128)(2,1)} copy(bf16[1,2,256,1024]{3,2,1,0:T(8,128)(2,1)} %bitcast.3) | data formatting | bytes 2097152

commit v2 on v1

--- a/solution.py
+++ b/solution.py
@@ -23,8 +23,10 @@
 WIDTH = 1024
 OWN = 32
 GROUP = 16
+GROUPS = OWN // GROUP
 HALO = 16
 TAPS = 7
+SPECTRUM, GATED, GATE, MIXED, EXCHANGES = 0, 1, 3, 5, 9
 
 
 def turn(numerator, period):
@@ -133,6 +135,20 @@
     spec_load = pltpu.make_async_copy(spectrum.at[:, 1, pl.ds(0, 256), :], spec_local, load_sem.at[0])
     proj_load = pltpu.make_async_copy(proj, proj_local.at[:, pl.ds(HALO, ROWS), :], load_sem.at[1])
     spec_load.start()
+    barrier = pltpu.get_barrier_semaphore()
+
+    @pl.loop(1, SHARDS)
+    def _(k):
+        pl.semaphore_signal(
+            barrier, inc=1, device_id={"seq": lax.rem(me + k, SHARDS)}, device_id_type=MESH
+        )
+
+    @pl.loop(1, CHANS)
+    def _(k):
+        pl.semaphore_signal(
+            barrier, inc=1, device_id={"chan": lax.rem(my_chan + k, CHANS)}, device_id_type=MESH
+        )
+
     proj_load.start()
     loads = [
         pltpu.make_async_copy(source, target, table_sem.at[index])
@@ -154,27 +170,6 @@
     for load in loads:
         load.start()
 
-    barrier = pltpu.get_barrier_semaphore()
-
-    @pl.loop(1, SHARDS)
-    def _(k):
-        pl.semaphore_signal(
-            barrier, inc=1, device_id={"seq": lax.rem(me + k, SHARDS)}, device_id_type=MESH
-        )
-
-    @pl.loop(1, CHANS)
-    def _(k):
-        pl.semaphore_signal(
-            barrier, inc=1, device_id={"chan": lax.rem(my_chan + k, CHANS)}, device_id_type=MESH
-        )
-
-    column = pl.multiple_of((me // 4) * 128, 128)
-    wide = jnp.transpose(jnp.broadcast_to(skip[:, pl.ds(column, 128)], (128, 128)))
-    unmixed[0, pl.ds(0, 128), pl.ds(0, 128)] = wide
-    mine = unmixed[0, pl.ds(pl.multiple_of(lax.rem(me, 4) * OWN, OWN), OWN), pl.ds(0, 128)]
-    skip_own[:, pl.ds(0, 128)] = mine
-    skip_own[:, pl.ds(128, 128)] = mine
-
     pl.semaphore_wait(barrier, SHARDS - 1 + CHANS - 1)
 
     halo = pltpu.make_async_remote_copy(
@@ -190,23 +185,20 @@
     def _():
         halo.start()
 
-    def own_rows(device):
-        return pl.ds(pl.multiple_of(device * OWN, OWN), OWN)
+    def send_one(source, target, device, which):
+        pltpu.make_async_remote_copy(
+            src_ref=source.at[device],
+            dst_ref=target.at[me],
+            send_sem=send_sem.at[which],
+            recv_sem=got_sem.at[which],
+            device_id={"seq": device},
+            device_id_type=MESH,
+        ).start()
 
     def send_all(source, target, which):
         @pl.loop(1, SHARDS)
         def _(k):
-            device = lax.rem(me + k, SHARDS)
-            pltpu.make_async_remote_copy(
-                src_ref=source.at[device],
-                dst_ref=target.at[me],
-                send_sem=send_sem.at[which],
-                recv_sem=got_sem.at[which],
-                device_id={"seq": device},
-                device_id_type=MESH,
-            ).start()
-
-        target[me] = source[me]
+            send_one(source, target, lax.rem(me + k, SHARDS), which)
 
     def wait_all(ref, sem):
         part = ref.at[pl.ds(0, SHARDS - 1)]
@@ -215,13 +207,29 @@
     spec_load.wait()
 
     @pl.loop(0, WIDTH // 128)
-    def _(block):
+    def _(step):
+        block = lax.rem(me // 4 + step, WIDTH // 128)
         columns = pl.ds(pl.multiple_of(block * 128, 128), 128)
         for part in range(2):
             value = jnp.transpose(spec_local[part, :, columns].astype(F32)).astype(BF16)
             spec_send[pl.ds(block * 4, 4), :, pl.ds(part * 256, 256)] = value.reshape(4, OWN, 256)
 
-    send_all(spec_send, spec_got, 0)
+        @pl.loop(0, 4)
+        def _(k):
+            device = block * 4 + lax.rem(me + k, 4)
+
+            @pl.when(device != me)
+            def _():
+                send_one(spec_send, spec_got, device, SPECTRUM)
+
+    spec_got[me] = spec_send[me]
+
+    column = pl.multiple_of((me // 4) * 128, 128)
+    wide = jnp.transpose(jnp.broadcast_to(skip[:, pl.ds(column, 128)], (128, 128)))
+    unmixed[pl.ds(0, 128), pl.ds(0, 128)] = wide
+    mine = unmixed[pl.ds(pl.multiple_of(lax.rem(me, 4) * OWN, OWN), OWN), pl.ds(0, 128)]
+    skip_own[:, pl.ds(0, 128)] = mine
+    skip_own[:, pl.ds(128, 128)] = mine
 
     proj_load.wait()
 
@@ -258,11 +266,16 @@
                 jnp.transpose(shorts[1] * shorts[2]).astype(BF16).reshape(4, OWN, 128)
             )
 
-    send_all(gated_send, gated_got, 1)
+    gated_got[me] = gated_send[me]
+    gate_got[me] = gate_send[me]
+    for group in range(GROUPS):
+        chans = pl.ds(group * GROUP, GROUP)
+        send_all(gated_send.at[:, chans, :], gated_got.at[:, chans, :], GATED + group)
+        send_all(gate_send.at[:, chans, :], gate_got.at[:, chans, :], GATE + group)
 
     for load in loads:
         load.wait()
-    wait_all(spec_got, got_sem.at[0])
+    wait_all(spec_got, got_sem.at[SPECTRUM])
 
     def turned(real, imag, cosine, sine, lanes, sign):
         real, imag = rows_of(real), rows_of(imag)
@@ -278,7 +291,7 @@
     uppers = (pl.ds(512, 256), pl.ds(768, 256))
     top, bottom = pl.ds(0, ROWS), pl.ds(ROWS, ROWS)
 
-    @pl.loop(0, OWN // GROUP)
+    @pl.loop(0, GROUPS)
     def _(group):
         chans = pl.ds(pl.multiple_of(group * GROUP, GROUP), GROUP)
         taken = spec_got[:, chans, :].reshape(ROWS, ROWS)
@@ -295,12 +308,10 @@
         for lanes in (*halves, *uppers):
             filter_freq[group, :, lanes] = dot(stacked_lanes[...], forward[:, lanes])
 
-    wait_all(gated_got, got_sem.at[1])
-    send_all(gate_send, gate_got, 2)
-
-    @pl.loop(0, OWN // GROUP)
+    @pl.loop(0, GROUPS)
     def _(group):
         chans = pl.ds(pl.multiple_of(group * GROUP, GROUP), GROUP)
+        wait_all(gated_got.at[:, chans, :], got_sem.at[GATED + group])
         for low, high in zip(halves, uppers):
             both = dot(outer_in[...], gated_got[:, chans, low].reshape(ROWS, 256))
             real, imag = turned(both[:ROWS], both[ROWS:], value_cos, value_sin, low, 1)
@@ -326,28 +337,31 @@
                 outer_out[:, bottom], stacked_lanes[:, high]
             )
             own = gated_got[:, chans, low].astype(F32)
-            unmixed[group, :, low] = (
+            unmixed[:, low] = (
                 value.reshape(SHARDS, GROUP, 256) + skip_own[chans, :][None] * own
             ).reshape(ROWS, 256)
 
-    wait_all(gate_got, got_sem.at[2])
-
-    for side in range(2):
-
-        @pl.loop(0, OWN // GROUP)
-        def _(group):
-            chans = pl.ds(pl.multiple_of(group * GROUP, GROUP), GROUP)
+        wait_all(gate_got.at[:, chans, :], got_sem.at[GATE + group])
+        for side in range(2):
             for half, lanes in enumerate(halves):
-                value = unmixed[group, pl.ds(side * 256, 256), lanes].reshape(16, GROUP, 256)
+                value = unmixed[pl.ds(side * 256, 256), lanes].reshape(16, GROUP, 256)
                 value = (gate_got[pl.ds(side * 16, 16), chans, lanes].astype(F32) * value).astype(BF16)
                 for index in range(16):
                     device = 2 * index + half if side == 0 else 31 - 2 * index - half
                     mixed_send[side, device, chans, :] = value[index]
-
-        send_all(mixed_send.at[side], mixed_got.at[side], 3 + side)
+            mixed_got[side, me, chans, :] = mixed_send[side, me, chans, :]
+            send_all(
+                mixed_send.at[side, :, chans, :],
+                mixed_got.at[side, :, chans, :],
+                MIXED + 2 * group + side,
+            )
 
     for side in range(2):
-        wait_all(mixed_got.at[side], got_sem.at[3 + side])
+        for group in range(GROUPS):
+            wait_all(
+                mixed_got.at[side, :, pl.ds(group * GROUP, GROUP), :],
+                got_sem.at[MIXED + 2 * group + side],
+            )
 
         def squares(block, total):
             value = mixed_got[side, pl.ds(block * 4, 4), :, :].astype(F32)
@@ -392,11 +406,14 @@
     def _():
         halo.wait_send()
 
-    wait_all(spec_send, send_sem.at[0])
-    wait_all(gated_send, send_sem.at[1])
-    wait_all(gate_send, send_sem.at[2])
+    wait_all(spec_send, send_sem.at[SPECTRUM])
+    for group in range(GROUPS):
+        chans = pl.ds(group * GROUP, GROUP)
+        wait_all(gated_send.at[:, chans, :], send_sem.at[GATED + group])
+        wait_all(gate_send.at[:, chans, :], send_sem.at[GATE + group])
+        for side in range(2):
+            wait_all(mixed_send.at[side, :, chans, :], send_sem.at[MIXED + 2 * group + side])
     for side in range(2):
-        wait_all(mixed_send.at[side], send_sem.at[3 + side])
         part = power_got.at[side, pl.ds(0, CHANS - 1)]
         pltpu.make_async_copy(part, part, power_send_sem.at[side]).wait()
 
@@ -424,18 +441,18 @@
             pltpu.VMEM((2, SHARDS, OWN, 256), BF16),
             pltpu.VMEM((2, SHARDS, OWN, 256), BF16),
             *held,
-            pltpu.VMEM((OWN // GROUP, ROWS, 2 * ROWS), F32),
+            pltpu.VMEM((GROUPS, ROWS, 2 * ROWS), F32),
             pltpu.VMEM((2 * ROWS, ROWS), BF16),
             pltpu.VMEM((ROWS, 2 * ROWS), BF16),
-            pltpu.VMEM((OWN // GROUP, ROWS, ROWS), F32),
+            pltpu.VMEM((ROWS, ROWS), F32),
             pltpu.VMEM((OWN, 256), F32),
             pltpu.VMEM((2, 8, 256), F32),
             pltpu.VMEM((2, CHANS, 8, 256), F32),
             pltpu.SemaphoreType.DMA((2,)),
             pltpu.SemaphoreType.DMA((len(constants),)),
             pltpu.SemaphoreType.DMA((2,)),
-            pltpu.SemaphoreType.DMA((5,)),
-            pltpu.SemaphoreType.DMA((5,)),
+            pltpu.SemaphoreType.DMA((EXCHANGES,)),
+            pltpu.SemaphoreType.DMA((EXCHANGES,)),
             pltpu.SemaphoreType.DMA((2,)),
             pltpu.SemaphoreType.DMA((2,)),
         ],

time: 122 us -> 112 us (0.918)
  Pallas kernels: 119 us -> 110 us
    pallas_call x1, Pallas kernels: 119 us -> 110 us  [body(): pl.pallas_call(kernel, out_shape=jax.ShapeDtypeStruct((ROWS, WIDTH), BF16...]
where the time goes in v2:
time: 112 us
  Pallas kernels  110 us (98%)
  local copies, waits for them, and re-layouts  2.26 us (2%)
    pallas_call x1, Pallas kernels, body(): pl.pallas_call(kernel, out_shape=jax.ShapeDtypeStruct((ROWS, WIDTH), BF16...  110 us
    unnamed x1, local copies, waits for them, and re-layouts  2.26 us

profile of v2, /device:TPU:1, one launch (start us, length us, event | category | flops | bytes accessed | tf_op | source)
XLA Modules:
  0.0 112.3 jit_solution(16992337811584764102)
XLA Ops:
  0.0 110.0 %shard_map.145 = bf16[512,1024]{1,0:T(8,128)(2,1)} custom-call(bf16[3,512,1024]{2,1,0:T(8,128)(2,1)} %proj.1, bf16[2,2,512,1024]{3,2,1,0:T(8,128)(2,1)} %spectrum.1, f32[3,7,1024]{2,1,0:T(8,128)} %weight.1, f32[1,1024]{1,0:T(1,128)} %bitcast.4, f32[1,1024]{1,0:T(1,128)} %bitcast.5, bf16[512,1024]{1,0:T(8,128)(2,1)} %constant.20.clone.h_spectrum_in, ...), custom_call_target="tpu_custom_call" | custom-call | tf_op jit(solution)/shard_map/pallas_call | solution.py:427
  110.0 2.3 %copy.17 = bf16[1,2,256,1024]{3,2,1,0:T(8,128)(2,1)} copy(bf16[1,2,256,1024]{3,2,1,0:T(8,128)(2,1)} %bitcast.3) | data formatting | bytes 2097152

commit v3 on v2

--- a/solution.py
+++ b/solution.py
@@ -26,7 +26,7 @@
 GROUPS = OWN // GROUP
 HALO = 16
 TAPS = 7
-SPECTRUM, GATED, GATE, MIXED, EXCHANGES = 0, 1, 3, 5, 9
+SPECTRUM, GATED, GATE, MIXED, POWER, EXCHANGES = 0, 1, 3, 5, 9, 10
 
 
 def turn(numerator, period):
@@ -80,9 +80,9 @@
 def kernel(
     proj,
     spectrum,
-    weight,
-    skip,
-    gain,
+    h_weight,
+    h_skip,
+    h_gain,
     h_spectrum_in,
     h_filter_outer,
     h_forward,
@@ -93,6 +93,10 @@
     h_filter_sin,
     h_value_cos,
     h_value_sin,
+    h_out,
+    weight,
+    skip,
+    gain,
     out,
     spec_local,
     proj_local,
@@ -119,15 +123,17 @@
     stacked_lanes,
     unmixed,
     skip_own,
+    part_send,
+    part_got,
     power_send,
     power_got,
+    scales,
     load_sem,
     table_sem,
     halo_sem,
     send_sem,
     got_sem,
-    power_send_sem,
-    power_got_sem,
+    power_sem,
 ):
     me = lax.axis_index("seq")
     my_chan = lax.axis_index("chan")
@@ -149,11 +155,49 @@
             barrier, inc=1, device_id={"chan": lax.rem(my_chan + k, CHANS)}, device_id_type=MESH
         )
 
+    pl.semaphore_wait(barrier, SHARDS - 1 + CHANS - 1)
+
+    halo = pltpu.make_async_remote_copy(
+        src_ref=proj.at[:, pl.ds(ROWS - HALO, HALO), :],
+        dst_ref=proj_local.at[:, pl.ds(0, HALO), :],
+        send_sem=halo_sem.at[0],
+        recv_sem=halo_sem.at[1],
+        device_id={"seq": lax.rem(me + 1, SHARDS)},
+        device_id_type=MESH,
+    )
+
+    @pl.when(me < SHARDS - 1)
+    def _():
+        halo.start()
+
+    def send_one(source, target, device, which):
+        pltpu.make_async_remote_copy(
+            src_ref=source.at[device],
+            dst_ref=target.at[me],
+            send_sem=send_sem.at[which],
+            recv_sem=got_sem.at[which],
+            device_id={"seq": device},
+            device_id_type=MESH,
+        ).start()
+
+    def send_all(source, target, which):
+        @pl.loop(1, SHARDS)
+        def _(k):
+            send_one(source, target, lax.rem(me + k, SHARDS), which)
+
+    def wait_all(ref, sem):
+        part = ref.at[pl.ds(0, SHARDS - 1)]
+        pltpu.make_async_copy(part, part, sem).wait()
+
+    spec_load.wait()
     proj_load.start()
     loads = [
         pltpu.make_async_copy(source, target, table_sem.at[index])
         for index, (source, target) in enumerate(
             (
+                (h_weight, weight),
+                (h_skip, skip),
+                (h_gain, gain),
                 (h_spectrum_in, spectrum_in),
                 (h_filter_outer, filter_outer),
                 (h_forward, forward),
@@ -170,42 +214,6 @@
     for load in loads:
         load.start()
 
-    pl.semaphore_wait(barrier, SHARDS - 1 + CHANS - 1)
-
-    halo = pltpu.make_async_remote_copy(
-        src_ref=proj.at[:, pl.ds(ROWS - HALO, HALO), :],
-        dst_ref=proj_local.at[:, pl.ds(0, HALO), :],
-        send_sem=halo_sem.at[0],
-        recv_sem=halo_sem.at[1],
-        device_id={"seq": lax.rem(me + 1, SHARDS)},
-        device_id_type=MESH,
-    )
-
-    @pl.when(me < SHARDS - 1)
-    def _():
-        halo.start()
-
-    def send_one(source, target, device, which):
-        pltpu.make_async_remote_copy(
-            src_ref=source.at[device],
-            dst_ref=target.at[me],
-            send_sem=send_sem.at[which],
-            recv_sem=got_sem.at[which],
-            device_id={"seq": device},
-            device_id_type=MESH,
-        ).start()
-
-    def send_all(source, target, which):
-        @pl.loop(1, SHARDS)
-        def _(k):
-            send_one(source, target, lax.rem(me + k, SHARDS), which)
-
-    def wait_all(ref, sem):
-        part = ref.at[pl.ds(0, SHARDS - 1)]
-        pltpu.make_async_copy(part, part, sem).wait()
-
-    spec_load.wait()
-
     @pl.loop(0, WIDTH // 128)
     def _(step):
         block = lax.rem(me // 4 + step, WIDTH // 128)
@@ -223,6 +231,9 @@
                 send_one(spec_send, spec_got, device, SPECTRUM)
 
     spec_got[me] = spec_send[me]
+
+    for load in loads[:3]:
+        load.wait()
 
     column = pl.multiple_of((me // 4) * 128, 128)
     wide = jnp.transpose(jnp.broadcast_to(skip[:, pl.ds(column, 128)], (128, 128)))
@@ -273,7 +284,7 @@
         send_all(gated_send.at[:, chans, :], gated_got.at[:, chans, :], GATED + group)
         send_all(gate_send.at[:, chans, :], gate_got.at[:, chans, :], GATE + group)
 
-    for load in loads:
+    for load in loads[3:]:
         load.wait()
     wait_all(spec_got, got_sem.at[SPECTRUM])
 
@@ -307,6 +318,8 @@
             stacked_lanes[:, high] = imag
         for lanes in (*halves, *uppers):
             filter_freq[group, :, lanes] = dot(stacked_lanes[...], forward[:, lanes])
+
+    part_send[...] = jnp.zeros(part_send.shape, F32)
 
     @pl.loop(0, GROUPS)
     def _(group):
@@ -346,9 +359,19 @@
             for half, lanes in enumerate(halves):
                 value = unmixed[pl.ds(side * 256, 256), lanes].reshape(16, GROUP, 256)
                 value = (gate_got[pl.ds(side * 16, 16), chans, lanes].astype(F32) * value).astype(BF16)
+                squares = value.astype(F32)
+                squares = (squares * squares).reshape(16, 2, 8, 256)
+                squares = jnp.sum(jnp.sum(squares, axis=1), axis=1, keepdims=True)
                 for index in range(16):
                     device = 2 * index + half if side == 0 else 31 - 2 * index - half
                     mixed_send[side, device, chans, :] = value[index]
+                    part_send[device, :, pl.ds(side * 256, 256)] += squares[index]
+
+        @pl.when(group == GROUPS - 1)
+        def _():
+            send_all(part_send, part_got, POWER)
+
+        for side in range(2):
             mixed_got[side, me, chans, :] = mixed_send[side, me, chans, :]
             send_all(
                 mixed_send.at[side, :, chans, :],
@@ -356,51 +379,52 @@
                 MIXED + 2 * group + side,
             )
 
+    stores = [
+        pltpu.make_async_copy(
+            out.at[pl.ds(side * 256, 256), :], h_out.at[pl.ds(side * 256, 256), :], load_sem.at[side]
+        )
+        for side in range(2)
+    ]
+    part_got[me] = part_send[me]
+    wait_all(part_got, got_sem.at[POWER])
+    power = jnp.sum(part_got[...], axis=0)
+    power_send[...] = power
+    power_got[my_chan] = power
+
+    @pl.loop(1, CHANS)
+    def _(k):
+        pltpu.make_async_remote_copy(
+            src_ref=power_send,
+            dst_ref=power_got.at[my_chan],
+            send_sem=power_sem.at[0],
+            recv_sem=power_sem.at[1],
+            device_id={"chan": lax.rem(my_chan + k, CHANS)},
+            device_id_type=MESH,
+        ).start()
+
+    others = power_got.at[pl.ds(0, CHANS - 1)]
+    pltpu.make_async_copy(others, others, power_sem.at[1]).wait()
+    scale = lax.rsqrt(jnp.sum(power_got[...], axis=0) * (1.0 / D) + EPSILON)
+    scales[...] = jnp.transpose(jnp.broadcast_to(scale, (128, ROWS)))
+
     for side in range(2):
+        rows = pl.ds(side * 256, 256)
         for group in range(GROUPS):
             wait_all(
                 mixed_got.at[side, :, pl.ds(group * GROUP, GROUP), :],
                 got_sem.at[MIXED + 2 * group + side],
             )
 
-        def squares(block, total):
-            value = mixed_got[side, pl.ds(block * 4, 4), :, :].astype(F32)
-            value = (value * value).reshape(16, 8, 256)
-            return total + jnp.sum(value, axis=0)
-
-        power = lax.fori_loop(0, WIDTH // 128, squares, jnp.zeros((8, 256), F32))
-        power_send[side] = power
-        power_got[side, my_chan] = power
-
-        @pl.loop(1, CHANS)
-        def _(k):
-            pltpu.make_async_remote_copy(
-                src_ref=power_send.at[side],
-                dst_ref=power_got.at[side, my_chan],
-                send_sem=power_send_sem.at[side],
-                recv_sem=power_got_sem.at[side],
-                device_id={"chan": lax.rem(my_chan + k, CHANS)},
-                device_id_type=MESH,
-            ).start()
-
         @pl.loop(0, WIDTH // 128)
         def _(block):
             value = mixed_got[side, pl.ds(block * 4, 4), :, :].reshape(128, 256).astype(F32)
             columns = pl.ds(pl.multiple_of(block * 128, 128), 128)
-            out[pl.ds(side * 256, 256), columns] = jnp.transpose(value).astype(BF16)
-
-    for side in range(2):
-        part = power_got.at[side, pl.ds(0, CHANS - 1)]
-        pltpu.make_async_copy(part, part, power_got_sem.at[side]).wait()
-        power = jnp.sum(jnp.sum(power_got[side], axis=0), axis=0, keepdims=True)
-        scale = lax.rsqrt(power * (1.0 / D) + EPSILON)
-        scale = jnp.transpose(jnp.broadcast_to(scale, (128, 256)))
-
-        @pl.loop(0, WIDTH // 128)
-        def _(block):
-            columns = pl.ds(pl.multiple_of(block * 128, 128), 128)
-            rows = pl.ds(side * 256, 256)
-            out[rows, columns] = (out[rows, columns].astype(F32) * scale * gain[:, columns]).astype(BF16)
+            out[rows, columns] = (jnp.transpose(value) * scales[rows, :] * gain[:, columns]).astype(BF16)
+
+        stores[side].start()
+
+    for store in stores:
+        store.wait()
 
     @pl.when(me < SHARDS - 1)
     def _():
@@ -413,9 +437,8 @@
         wait_all(gate_send.at[:, chans, :], send_sem.at[GATE + group])
         for side in range(2):
             wait_all(mixed_send.at[side, :, chans, :], send_sem.at[MIXED + 2 * group + side])
-    for side in range(2):
-        part = power_got.at[side, pl.ds(0, CHANS - 1)]
-        pltpu.make_async_copy(part, part, power_send_sem.at[side]).wait()
+    wait_all(part_send, send_sem.at[POWER])
+    pltpu.make_async_copy(others, others, power_sem.at[0]).wait()
 
 
 def body(proj, short_weight, spectrum, skip, gain):
@@ -423,13 +446,16 @@
     held = [pltpu.VMEM(c.shape, c.dtype) for c in constants]
     whole = (SHARDS, OWN, ROWS)
     anywhere = pl.BlockSpec(memory_space=pl.ANY)
-    inside = pl.BlockSpec(memory_space=pltpu.VMEM)
     value = pl.pallas_call(
         kernel,
         out_shape=jax.ShapeDtypeStruct((ROWS, WIDTH), BF16),
-        in_specs=[anywhere, anywhere, inside, inside, inside] + [anywhere] * len(constants),
-        out_specs=inside,
+        in_specs=[anywhere] * (5 + len(constants)),
+        out_specs=anywhere,
         scratch_shapes=[
+            pltpu.VMEM((3, TAPS, WIDTH), F32),
+            pltpu.VMEM((1, WIDTH), F32),
+            pltpu.VMEM((1, WIDTH), F32),
+            pltpu.VMEM((ROWS, WIDTH), BF16),
             pltpu.VMEM((2, 256, WIDTH), BF16),
             pltpu.VMEM((3, HALO + ROWS, WIDTH), BF16),
             pltpu.VMEM(whole, BF16),
@@ -446,14 +472,16 @@
             pltpu.VMEM((ROWS, 2 * ROWS), BF16),
             pltpu.VMEM((ROWS, ROWS), F32),
             pltpu.VMEM((OWN, 256), F32),
-            pltpu.VMEM((2, 8, 256), F32),
-            pltpu.VMEM((2, CHANS, 8, 256), F32),
+            pltpu.VMEM((SHARDS, 1, ROWS), F32),
+            pltpu.VMEM((SHARDS, 1, ROWS), F32),
+            pltpu.VMEM((1, ROWS), F32),
+            pltpu.VMEM((CHANS, 1, ROWS), F32),
+            pltpu.VMEM((ROWS, 128), F32),
             pltpu.SemaphoreType.DMA((2,)),
-            pltpu.SemaphoreType.DMA((len(constants),)),
+            pltpu.SemaphoreType.DMA((3 + len(constants),)),
             pltpu.SemaphoreType.DMA((2,)),
             pltpu.SemaphoreType.DMA((EXCHANGES,)),
             pltpu.SemaphoreType.DMA((EXCHANGES,)),
-            pltpu.SemaphoreType.DMA((2,)),
             pltpu.SemaphoreType.DMA((2,)),
         ],
         compiler_params=pltpu.CompilerParams(

time: 112 us -> 109 us (0.973)
  Pallas kernels: 110 us -> 107 us
    pallas_call x1, Pallas kernels: 110 us -> 107 us  [body(): pl.pallas_call(kernel, out_shape=jax.ShapeDtypeStruct((ROWS, WIDTH), BF16...]
where the time goes in v3:
time: 109 us
  Pallas kernels  107 us (98%)
  local copies, waits for them, and re-layouts  2.26 us (2%)
    pallas_call x1, Pallas kernels, body(): pl.pallas_call(kernel, out_shape=jax.ShapeDtypeStruct((ROWS, WIDTH), BF16...  107 us
    unnamed x1, local copies, waits for them, and re-layouts  2.26 us

profile of v3, /device:TPU:1, one launch (start us, length us, event | category | flops | bytes accessed | tf_op | source)
XLA Modules:
  0.0 109.1 jit_solution(15132227129517810431)
XLA Ops:
  0.0 106.8 %shard_map.145 = bf16[512,1024]{1,0:T(8,128)(2,1)} custom-call(bf16[3,512,1024]{2,1,0:T(8,128)(2,1)} %proj.1, bf16[2,2,512,1024]{3,2,1,0:T(8,128)(2,1)} %spectrum.1, f32[3,7,1024]{2,1,0:T(8,128)} %h_weight.1, f32[1,1024]{1,0:T(1,128)} %bitcast.4, f32[1,1024]{1,0:T(1,128)} %bitcast.5, bf16[512,1024]{1,0:T(8,128)(2,1)} %constant.20.clone.h_spectrum_in, ...), custom_call_target="tpu_custom_call" | custom-call | tf_op jit(solution)/shard_map/pallas_call | solution.py:449
  106.8 2.3 %copy.17 = bf16[1,2,256,1024]{3,2,1,0:T(8,128)(2,1)} copy(bf16[1,2,256,1024]{3,2,1,0:T(8,128)(2,1)} %bitcast.3) | data formatting | bytes 2097152

commit v4 on v3

--- a/solution.py
+++ b/solution.py
@@ -25,8 +25,9 @@
 GROUP = 16
 GROUPS = OWN // GROUP
 HALO = 16
+FINISH = 512
 TAPS = 7
-SPECTRUM, GATED, GATE, MIXED, POWER, EXCHANGES = 0, 1, 3, 5, 9, 10
+SPECTRUM, GATED, GATE, MIXED, POWER, EXCHANGES = 0, 1, 3, 5, 7, 8
 
 
 def turn(numerator, period):
@@ -82,7 +83,6 @@
     spectrum,
     h_weight,
     h_skip,
-    h_gain,
     h_spectrum_in,
     h_filter_outer,
     h_forward,
@@ -93,11 +93,10 @@
     h_filter_sin,
     h_value_cos,
     h_value_sin,
-    h_out,
+    mixed_got,
+    h_scales,
     weight,
     skip,
-    gain,
-    out,
     spec_local,
     proj_local,
     spec_send,
@@ -107,7 +106,6 @@
     gated_got,
     gate_got,
     mixed_send,
-    mixed_got,
     spectrum_in,
     filter_outer,
     forward,
@@ -134,6 +132,7 @@
     send_sem,
     got_sem,
     power_sem,
+    own_sem,
 ):
     me = lax.axis_index("seq")
     my_chan = lax.axis_index("chan")
@@ -197,7 +196,6 @@
             (
                 (h_weight, weight),
                 (h_skip, skip),
-                (h_gain, gain),
                 (h_spectrum_in, spectrum_in),
                 (h_filter_outer, filter_outer),
                 (h_forward, forward),
@@ -232,7 +230,7 @@
 
     spec_got[me] = spec_send[me]
 
-    for load in loads[:3]:
+    for load in loads[:2]:
         load.wait()
 
     column = pl.multiple_of((me // 4) * 128, 128)
@@ -284,7 +282,7 @@
         send_all(gated_send.at[:, chans, :], gated_got.at[:, chans, :], GATED + group)
         send_all(gate_send.at[:, chans, :], gate_got.at[:, chans, :], GATE + group)
 
-    for load in loads[3:]:
+    for load in loads[2:]:
         load.wait()
     wait_all(spec_got, got_sem.at[SPECTRUM])
 
@@ -318,6 +316,12 @@
             stacked_lanes[:, high] = imag
         for lanes in (*halves, *uppers):
             filter_freq[group, :, lanes] = dot(stacked_lanes[...], forward[:, lanes])
+
+    def own_store(group):
+        chans = pl.ds(pl.multiple_of(group * GROUP, GROUP), GROUP)
+        return pltpu.make_async_copy(
+            mixed_send.at[me, chans, :], mixed_got.at[me, chans, :], own_sem.at[group]
+        )
 
     part_send[...] = jnp.zeros(part_send.shape, F32)
 
@@ -364,27 +368,16 @@
                 squares = jnp.sum(jnp.sum(squares, axis=1), axis=1, keepdims=True)
                 for index in range(16):
                     device = 2 * index + half if side == 0 else 31 - 2 * index - half
-                    mixed_send[side, device, chans, :] = value[index]
+                    mixed_send[device, chans, pl.ds(side * 256, 256)] = value[index]
                     part_send[device, :, pl.ds(side * 256, 256)] += squares[index]
 
         @pl.when(group == GROUPS - 1)
         def _():
             send_all(part_send, part_got, POWER)
 
-        for side in range(2):
-            mixed_got[side, me, chans, :] = mixed_send[side, me, chans, :]
-            send_all(
-                mixed_send.at[side, :, chans, :],
-                mixed_got.at[side, :, chans, :],
-                MIXED + 2 * group + side,
-            )
-
-    stores = [
-        pltpu.make_async_copy(
-            out.at[pl.ds(side * 256, 256), :], h_out.at[pl.ds(side * 256, 256), :], load_sem.at[side]
-        )
-        for side in range(2)
-    ]
+        own_store(group).start()
+        send_all(mixed_send.at[:, chans, :], mixed_got.at[:, chans, :], MIXED + group)
+
     part_got[me] = part_send[me]
     wait_all(part_got, got_sem.at[POWER])
     power = jnp.sum(part_got[...], axis=0)
@@ -404,27 +397,14 @@
 
     others = power_got.at[pl.ds(0, CHANS - 1)]
     pltpu.make_async_copy(others, others, power_sem.at[1]).wait()
-    scale = lax.rsqrt(jnp.sum(power_got[...], axis=0) * (1.0 / D) + EPSILON)
-    scales[...] = jnp.transpose(jnp.broadcast_to(scale, (128, ROWS)))
-
-    for side in range(2):
-        rows = pl.ds(side * 256, 256)
-        for group in range(GROUPS):
-            wait_all(
-                mixed_got.at[side, :, pl.ds(group * GROUP, GROUP), :],
-                got_sem.at[MIXED + 2 * group + side],
-            )
-
-        @pl.loop(0, WIDTH // 128)
-        def _(block):
-            value = mixed_got[side, pl.ds(block * 4, 4), :, :].reshape(128, 256).astype(F32)
-            columns = pl.ds(pl.multiple_of(block * 128, 128), 128)
-            out[rows, columns] = (jnp.transpose(value) * scales[rows, :] * gain[:, columns]).astype(BF16)
-
-        stores[side].start()
-
-    for store in stores:
-        store.wait()
+    scales[...] = lax.rsqrt(jnp.sum(power_got[...], axis=0) * (1.0 / D) + EPSILON)
+
+    store = pltpu.make_async_copy(scales, h_scales, load_sem.at[0])
+    store.start()
+    for group in range(GROUPS):
+        wait_all(mixed_got.at[:, pl.ds(group * GROUP, GROUP), :], got_sem.at[MIXED + group])
+        own_store(group).wait()
+    store.wait()
 
     @pl.when(me < SHARDS - 1)
     def _():
@@ -435,10 +415,37 @@
         chans = pl.ds(group * GROUP, GROUP)
         wait_all(gated_send.at[:, chans, :], send_sem.at[GATED + group])
         wait_all(gate_send.at[:, chans, :], send_sem.at[GATE + group])
-        for side in range(2):
-            wait_all(mixed_send.at[side, :, chans, :], send_sem.at[MIXED + 2 * group + side])
+        wait_all(mixed_send.at[:, chans, :], send_sem.at[MIXED + group])
     wait_all(part_send, send_sem.at[POWER])
     pltpu.make_async_copy(others, others, power_sem.at[0]).wait()
+
+
+def finish(h_mixed, h_scales, h_gain, h_out, mixed, scales, gain, out, load_sem, store_sem):
+    steps = WIDTH // FINISH
+    loads, stores = [], []
+    for step in range(steps):
+        owners = pl.ds(step * FINISH // OWN, FINISH // OWN)
+        columns = pl.ds(step * FINISH, FINISH)
+        loads.append(pltpu.make_async_copy(h_mixed.at[owners], mixed.at[owners], load_sem.at[step]))
+        stores.append(pltpu.make_async_copy(out.at[:, columns], h_out.at[:, columns], store_sem.at[step]))
+    small = [
+        pltpu.make_async_copy(h_scales, scales, load_sem.at[steps]),
+        pltpu.make_async_copy(h_gain, gain, load_sem.at[steps + 1]),
+    ]
+    for load in small + loads:
+        load.start()
+    for load in small:
+        load.wait()
+    for step in range(steps):
+        loads[step].wait()
+        for block in range(step * FINISH // 128, (step + 1) * FINISH // 128):
+            columns = pl.ds(block * 128, 128)
+            value = mixed[pl.ds(block * 4, 4), :, :].reshape(128, ROWS).astype(F32)
+            value = jnp.transpose(value * scales[...])
+            out[:, columns] = (value * gain[:, columns]).astype(BF16)
+        stores[step].start()
+    for store in stores:
+        store.wait()
 
 
 def body(proj, short_weight, spectrum, skip, gain):
@@ -446,16 +453,17 @@
     held = [pltpu.VMEM(c.shape, c.dtype) for c in constants]
     whole = (SHARDS, OWN, ROWS)
     anywhere = pl.BlockSpec(memory_space=pl.ANY)
-    value = pl.pallas_call(
+    mixed, scales = pl.pallas_call(
         kernel,
-        out_shape=jax.ShapeDtypeStruct((ROWS, WIDTH), BF16),
-        in_specs=[anywhere] * (5 + len(constants)),
-        out_specs=anywhere,
+        out_shape=(
+            jax.ShapeDtypeStruct(whole, BF16),
+            jax.ShapeDtypeStruct((1, ROWS), F32),
+        ),
+        in_specs=[anywhere] * (4 + len(constants)),
+        out_specs=(anywhere, anywhere),
         scratch_shapes=[
             pltpu.VMEM((3, TAPS, WIDTH), F32),
             pltpu.VMEM((1, WIDTH), F32),
-            pltpu.VMEM((1, WIDTH), F32),
-            pltpu.VMEM((ROWS, WIDTH), BF16),
             pltpu.VMEM((2, 256, WIDTH), BF16),
             pltpu.VMEM((3, HALO + ROWS, WIDTH), BF16),
             pltpu.VMEM(whole, BF16),
@@ -464,8 +472,7 @@
             pltpu.VMEM(whole, BF16),
             pltpu.VMEM(whole, BF16),
             pltpu.VMEM(whole, BF16),
-            pltpu.VMEM((2, SHARDS, OWN, 256), BF16),
-            pltpu.VMEM((2, SHARDS, OWN, 256), BF16),
+            pltpu.VMEM(whole, BF16),
             *held,
             pltpu.VMEM((GROUPS, ROWS, 2 * ROWS), F32),
             pltpu.VMEM((2 * ROWS, ROWS), BF16),
@@ -476,18 +483,33 @@
             pltpu.VMEM((SHARDS, 1, ROWS), F32),
             pltpu.VMEM((1, ROWS), F32),
             pltpu.VMEM((CHANS, 1, ROWS), F32),
-            pltpu.VMEM((ROWS, 128), F32),
+            pltpu.VMEM((1, ROWS), F32),
             pltpu.SemaphoreType.DMA((2,)),
-            pltpu.SemaphoreType.DMA((3 + len(constants),)),
+            pltpu.SemaphoreType.DMA((2 + len(constants),)),
             pltpu.SemaphoreType.DMA((2,)),
             pltpu.SemaphoreType.DMA((EXCHANGES,)),
             pltpu.SemaphoreType.DMA((EXCHANGES,)),
             pltpu.SemaphoreType.DMA((2,)),
+            pltpu.SemaphoreType.DMA((GROUPS,)),
         ],
         compiler_params=pltpu.CompilerParams(
             collective_id=0, has_side_effects=True, vmem_limit_bytes=56 * 2**20
         ),
-    )(proj, spectrum, short_weight, skip[None], gain[None], *(jnp.asarray(c) for c in constants))
+    )(proj, spectrum, short_weight, skip[None], *(jnp.asarray(c) for c in constants))
+    value = pl.pallas_call(
+        finish,
+        out_shape=jax.ShapeDtypeStruct((ROWS, WIDTH), BF16),
+        in_specs=[anywhere] * 3,
+        out_specs=anywhere,
+        scratch_shapes=[
+            pltpu.VMEM(whole, BF16),
+            pltpu.VMEM((1, ROWS), F32),
+            pltpu.VMEM((1, WIDTH), F32),
+            pltpu.VMEM((ROWS, WIDTH), BF16),
+            pltpu.SemaphoreType.DMA((WIDTH // FINISH + 2,)),
+            pltpu.SemaphoreType.DMA((WIDTH // FINISH,)),
+        ],
+    )(mixed, scales, gain[None])
     return value.reshape(1, 2, ROWS // 2, WIDTH)
 
 

time: 109 us -> 108 us (level)
  local copies, waits for them, and re-layouts: 2.26 us -> 0 us
    unnamed x1 -> x0, local copies, waits for them, and re-layouts: 2.26 us -> none
    pallas_call x1 -> x2, Pallas kernels: 107 us -> 108 us  [the longest x1 105 us: body(): pl.pallas_call(kernel, out_shape=(jax.ShapeDtypeStruct(whole, BF16), jax....]
where the time goes in v4:
time: 108 us
  Pallas kernels  108 us (100%)
    pallas_call x1, Pallas kernels, body(): pl.pallas_call(kernel, out_shape=(jax.ShapeDtypeStruct(whole, BF16), jax....  105 us
    pallas_call x1, Pallas kernels, body(): pl.pallas_call(finish, out_shape=jax.ShapeDtypeStruct((ROWS, WIDTH), BF16...  2.59 us

profile of v4, /device:TPU:1, one launch (start us, length us, event | category | flops | bytes accessed | tf_op | source)
XLA Modules:
  0.0 107.6 jit_solution(12446938936541858438)
XLA Ops:
  0.0 105.0 %shard_map.145 = (bf16[32,32,512]{2,1,0:T(8,128)(2,1)}, f32[1,512]{1,0:T(1,128)}) custom-call(bf16[3,512,1024]{2,1,0:T(8,128)(2,1)} %proj.1, bf16[2,2,512,1024]{3,2,1,0:T(8,128)(2,1)} %spectrum.1, f32[3,7,1024]{2,1,0:T(8,128)} %h_weight.1, f32[1,1024]{1,0:T(1,128)} %bitcast.4, bf16[512,1024]{1,0:T(8,128)(2,1)} %constant.20.clone.h_spectrum_in, ...), custom_call_target="tpu_custom_call" | custom-call | tf_op jit(solution)/shard_map/pallas_call | solution.py:456
  105.0 2.6 %shard_map.146 = bf16[512,1024]{1,0:T(8,128)(2,1)} custom-call(bf16[32,32,512]{2,1,0:T(8,128)(2,1)} %get-tuple-element.7.h_mixed, f32[1,512]{1,0:T(1,128)} %get-tuple-element.8.h_scales, f32[1,1024]{1,0:T(1,128)} %bitcast.3), custom_call_target="tpu_custom_call" | custom-call | tf_op jit(solution)/shard_map/pallas_call | solution.py:499

commit v5 on v4

--- a/solution.py
+++ b/solution.py
@@ -25,7 +25,7 @@
 GROUP = 16
 GROUPS = OWN // GROUP
 HALO = 16
-FINISH = 512
+FINISH = 256
 TAPS = 7
 SPECTRUM, GATED, GATE, MIXED, POWER, EXCHANGES = 0, 1, 3, 5, 7, 8
 

time: 108 us -> 108 us (level)
  no operation moved by 1% of the time
where the time goes in v5:
time: 108 us
  Pallas kernels  108 us (100%)
    pallas_call x1, Pallas kernels, body(): pl.pallas_call(kernel, out_shape=(jax.ShapeDtypeStruct(whole, BF16), jax....  105 us
    pallas_call x1, Pallas kernels, body(): pl.pallas_call(finish, out_shape=jax.ShapeDtypeStruct((ROWS, WIDTH), BF16...  2.59 us

profile of v5, /device:TPU:1, one launch (start us, length us, event | category | flops | bytes accessed | tf_op | source)
XLA Modules:
  0.0 107.6 jit_solution(3039331290200976866)
XLA Ops:
  0.0 105.0 %shard_map.145 = (bf16[32,32,512]{2,1,0:T(8,128)(2,1)}, f32[1,512]{1,0:T(1,128)}) custom-call(bf16[3,512,1024]{2,1,0:T(8,128)(2,1)} %proj.1, bf16[2,2,512,1024]{3,2,1,0:T(8,128)(2,1)} %spectrum.1, f32[3,7,1024]{2,1,0:T(8,128)} %h_weight.1, f32[1,1024]{1,0:T(1,128)} %bitcast.4, bf16[512,1024]{1,0:T(8,128)(2,1)} %constant.20.clone.h_spectrum_in, ...), custom_call_target="tpu_custom_call" | custom-call | tf_op jit(solution)/shard_map/pallas_call | solution.py:456
  105.0 2.6 %shard_map.146 = bf16[512,1024]{1,0:T(8,128)(2,1)} custom-call(bf16[32,32,512]{2,1,0:T(8,128)(2,1)} %get-tuple-element.7.h_mixed, f32[1,512]{1,0:T(1,128)} %get-tuple-element.8.h_scales, f32[1,1024]{1,0:T(1,128)} %bitcast.3), custom_call_target="tpu_custom_call" | custom-call | tf_op jit(solution)/shard_map/pallas_call | solution.py:499
